TPU v7x, 32 devices: a whole 2x2x4 slice. The times are simulated.
32 devices in a mesh: groups: 2 (over y), row: 4 (over z), col: 4 (over x, core).
Axes of the slice: x: 2, y: 2, z: 4, core: 2. Of those that a mesh axis runs over, the one named last changes fastest.
Arguments:
- positions: float32 [4096, 3, 128], P(('groups', 'row', 'col')), parts along dimension 0, may hold values from -6 to 6
- normals: float32 [4096, 3, 128], P(('groups', 'row', 'col')), parts along dimension 0, may hold values from -6 to 6
- curvature: float32 [4096, 128], P(('groups', 'row', 'col')), parts along dimension 0, may hold values from 0.5 to 3
- pair_targets: int32 [32, 512], P(('groups', 'row', 'col')), parts along dimension 0, may hold values from 0 to 511, as said below
- pair_sources: int32 [32, 512], P(('groups', 'row', 'col')), parts along dimension 0, may hold values from 0 to 511
- pair_count: int32 [32], P(('groups', 'row', 'col')), parts along dimension 0, may hold values from 64 to 512, as said below
- node_counts: int32 [512, 8], P('groups'), parts along dimension 0, may hold values from 1 to 128, 642 in all within a row
- drop_clusters: int32 [512, 8], P('groups'), parts along dimension 0, may hold values from 0 to 2047, as said below
- drop_owner: int32 [512], P('groups'), parts along dimension 0, may hold values from 0 to 15, as said below
Outputs:
- drop_velocity: float32 [4096, 3, 128], P(('groups', 'row', 'col')), parts along dimension 0
There are 2 independent parts, one for each index of `groups`. A program takes and returns all parts, laid end to end along the dimension named above; each array names one. Nothing has to cross between parts.
Inputs may be any that keep to these rules, and one draw needn't show every extreme that they name: `drop_clusters`: every cluster of 0 to 2047 appears exactly once. Of the 128 clusters of one device, at most 16 belong to drops of any one owner, and this many is reached. `drop_owner`: every device owns exactly 16 drops. `pair_count`: the largest count is reached on some device; list entries past a device's count are not pairs. In each device's list, at most 256 entries have the same value of pair_targets // 128, and every device's list reaches this many for some value. `node_counts`: each drop's counts sum to 642.
All inputs are finite; a program needn't handle non-finite values.
Results may differ from a plain program's by a relative error of at most 0.0003.
Values sent between devices are 32-bit elements; how exact they have to be, the bound alone decides.
A program may use at most 64 MiB of HBM per device.

v0:
```python
import math

import jax
import jax.numpy as jnp
from jax import lax
from jax.sharding import PartitionSpec as P

pair_block = 32
regular_sq = 0.0025
stokes_scale = 1.0 / (8.0 * math.pi)


def stokeslet(target_pos, source_pos, source_force):
    delta_x = target_pos[:, 0, :, None] - source_pos[:, 0, None, :]
    delta_y = target_pos[:, 1, :, None] - source_pos[:, 1, None, :]
    delta_z = target_pos[:, 2, :, None] - source_pos[:, 2, None, :]
    dist_sq = delta_x * delta_x + delta_y * delta_y + delta_z * delta_z
    inverse = lax.rsqrt(dist_sq + regular_sq)
    weight = inverse * inverse * inverse
    isotropic = (dist_sq + 2.0 * regular_sq) * weight
    force_x = source_force[:, 0, None, :]
    force_y = source_force[:, 1, None, :]
    force_z = source_force[:, 2, None, :]
    project = (delta_x * force_x + delta_y * force_y + delta_z * force_z) * weight
    speed_x = jnp.sum(isotropic * force_x + project * delta_x, axis=2)
    speed_y = jnp.sum(isotropic * force_y + project * delta_y, axis=2)
    speed_z = jnp.sum(isotropic * force_z + project * delta_z, axis=2)
    return stokes_scale * jnp.stack([speed_x, speed_y, speed_z], axis=1)


def per_device(
    positions,
    normals,
    curvature,
    pair_targets,
    pair_sources,
    pair_count,
    node_counts,
    drop_clusters,
    drop_owner,
):
    local_count = positions.shape[0]
    node_slots = positions.shape[2]
    row_size = lax.axis_size("row")
    col_size = lax.axis_size("col")
    device_total = row_size * col_size
    device = lax.axis_index("row") * col_size + lax.axis_index("col")
    capacity = max(2, 2 * local_count // device_total)
    per_drop = drop_clusters.shape[1]
    drops_here = local_count // per_drop
    flat_clusters = drop_clusters.reshape(-1)
    flat_counts = node_counts.reshape(-1)
    entries = flat_clusters.shape[0]
    inverse_map = (
        jnp.zeros((entries,), jnp.int32).at[flat_clusters].set(jnp.arange(entries, dtype=jnp.int32))
    )
    home_entry = lax.dynamic_slice_in_dim(inverse_map, device * local_count, local_count)
    home_counts = flat_counts[home_entry]
    slot_index = jnp.arange(node_slots, dtype=jnp.int32)
    home_live = (slot_index[None, :] < home_counts[:, None]).astype(jnp.float32)
    forces = (curvature * home_live)[:, None, :] * normals
    targets = lax.all_gather(positions, "col", axis=0, tiled=True)
    source_pos, source_force = (
        lax.all_gather(positions, "row", axis=0, tiled=True),
        lax.all_gather(forces, "row", axis=0, tiled=True),
    )
    target_rows = targets.shape[0]
    pair_slots = pair_targets.shape[1]
    valid = jnp.arange(pair_slots, dtype=jnp.int32) < pair_count[0]
    sort_keys = jnp.where(valid, pair_targets[0], target_rows)
    ordering = jnp.argsort(sort_keys, stable=True)
    sorted_targets = sort_keys[ordering]
    sorted_sources = pair_sources[0][ordering]
    first = jnp.sum(sorted_targets < 0)
    beyond = jnp.sum(sorted_targets < 0 + target_rows)
    blocks = (beyond - first + pair_block - 1) // pair_block

    def accumulate(block_number, totals):
        picked = first + block_number * pair_block + jnp.arange(pair_block, dtype=jnp.int32)
        active = picked < beyond
        picked = jnp.minimum(picked, pair_slots - 1)
        target_ids = jnp.minimum(sorted_targets[picked], target_rows - 1)
        source_ids = sorted_sources[picked]
        speeds = stokeslet(targets[target_ids], source_pos[source_ids], source_force[source_ids])
        speeds = speeds * active.astype(jnp.float32)[:, None, None]
        offsets = jnp.clip(target_ids - 0, 0, target_rows - 1)
        return totals.at[offsets].add(speeds)

    home_speed = lax.psum_scatter(
        lax.fori_loop(0, blocks, accumulate, jnp.zeros((target_rows, 3, node_slots), jnp.float32)),
        "col",
        scatter_dimension=0,
        tiled=True,
    )
    home_owner = drop_owner[home_entry // per_drop]
    local_order = jnp.arange(local_count, dtype=jnp.int32)
    earlier = (home_owner[None, :] == home_owner[:, None]) & (
        local_order[None, :] < local_order[:, None]
    )
    send_rank = jnp.sum(earlier, axis=1)
    outgoing = jnp.zeros((device_total * capacity, 3, node_slots), jnp.float32)
    outgoing = outgoing.at[home_owner * capacity + send_rank].set(home_speed)
    arrived = lax.all_to_all(outgoing, ("row", "col"), split_axis=0, concat_axis=0, tiled=True)
    owner_order = jnp.argsort(drop_owner, stable=True)
    owned = lax.dynamic_slice_in_dim(owner_order, device * drops_here, drops_here)
    owned_clusters = drop_clusters[owned].reshape(-1)
    owned_counts = node_counts[owned].reshape(-1)
    anchor = owned_clusters // local_count
    before = (anchor[None, :] == anchor[:, None]) & (
        owned_clusters[None, :] < owned_clusters[:, None]
    )
    arrive_rank = jnp.sum(before, axis=1)
    owned_live = (slot_index[None, :] < owned_counts[:, None]).astype(jnp.float32)
    return arrived[anchor * capacity + arrive_rank] * owned_live[:, None, :]


def solution(mesh):
    in_specs = (
        P(("groups", "row", "col"), None, None),
        P(("groups", "row", "col"), None, None),
        P(("groups", "row", "col"), None),
        P(("groups", "row", "col"), None),
        P(("groups", "row", "col"), None),
        P(("groups", "row", "col")),
        P("groups", None),
        P("groups", None),
        P("groups"),
    )
    out_specs = P(("groups", "row", "col"), None, None)
    return jax.shard_map(
        per_device, mesh=mesh, in_specs=in_specs, out_specs=out_specs, check_vma=False
    )
```

profile of v0, /device:TPU:15, one launch (start us, length us, event | category | flops | bytes accessed | tf_op | source)
XLA Modules:
  0.0 376.8 jit_solution(6808647549697550242)
XLA Ops:
  7.9 3.8 %sort.34 = (s32[512]{0:T(512)}, s32[512]{0:T(512)S(1)}) sort(s32[512]{0:T(512)S(1)} %fusion.24, s32[512]{0:T(512)S(1)} %iota.36), dimensions={0}, to_apply=%region_2.3 | sort | flops 4608 | bytes 8192 | tf_op jit(solution)/shard_map/jit(argsort)/sort | solution.py:71
  11.7 3.5 gather_fusion.6
  17.1 8.7 %all_gather.9 = f32[512,3,128]{2,0,1:T(8,128)S(1)} all-gather(f32[128,3,128]{2,0,1:T(8,128)S(1)} %copy-done.3), channel_id=1, replica_groups=mesh['groups'=2,'row'=4,'col'=4] {'col'}, dimensions={0}, use_global_device_ids=true | all-gather | bytes 983040 | tf_op jit(solution)/shard_map/all_gather | solution.py:62
  25.8 17.0 %all_gather.10 = f32[512,3,128]{2,0,1:T(8,128)S(1)} all-gather(f32[128,3,128]{2,0,1:T(8,128)S(1)} %copy-done.3), channel_id=1, replica_groups=mesh['groups'=2,'row'=4,'col'=4] {'row'}, dimensions={0}, use_global_device_ids=true | all-gather | bytes 983040 | tf_op jit(solution)/shard_map/all_gather | solution.py:64
  43.3 8.0 %scatter_custom_fusion.1 = s32[2048]{0:T(1024)S(1)} fusion(s32[2048]{0:T(1024)S(1)} %bitcast.89, s32[2048]{0:T(1024)S(1)} %iota.34, s32[]{:T(128)} %constant.80.clone.1), kind=kCustom, calls=%fused_computation.70 | custom fusion | bytes 8196 | tf_op jit(solution)/shard_map/scatter | solution.py:55
  52.1 1.1 gather_fusion.8
  53.3 16.0 %all_gather.11 = f32[512,3,128]{2,0,1:T(8,128)S(1)} all-gather(f32[128,3,128]{2,0,1:T(8,128)S(1)} %broadcast_multiply_fusion.1), channel_id=1, replica_groups=mesh['groups'=2,'row'=4,'col'=4] {'row'}, dimensions={0}, use_global_device_ids=true | all-gather | bytes 983040 | tf_op jit(solution)/shard_map/all_gather | solution.py:65
  69.9 3.5 gather_fusion.7
  73.4 1.5 copy.42
  75.6 82.1 %while.10 = (s32[]{:T(128)}, f32[512,3,128]{2,1,0:T(4,128)S(1)}, s32[]{:T(128)}, s32[]{:T(128)}, s32[512]{0:T(512)S(1)}, /*index=5*/f32[512,3,128]{2,1,0:T(4,128...) while((s32[]{:T(128)}, f32[512,3,128]{2,1,0:T(4,128)S(1)}, ...), condition=%wide.region_10.11_spmd, body=%wide.region_5.10_spmd.sunk | while | flops 16293508 | bytes 1145625 | solution.py:90
  76.2 0.7 gather_fusion
  77.5 1.8 gather_fusion.4
  79.4 0.7 gather_fusion.1
  82.1 4.7 %fusion.43 = (f32[32,128]{1,0:T(8,128)S(1)}, f32[32,128]{1,0:T(8,128)S(1)}, f32[32,128]{1,0:T(8,128)S(1)}) fusion(f32[32,128]{1,0:T(8,128)} %bitcast.81, f32[32,128]{1,0:T(8,128)S(1)} %bitcast.84, f32[32,128]{1,0:T(8,128)S(1)} %bitcast.78, f32[32,128]{1,0:T(8,128)S(1)} %bitcast.85, f32[32,128]{1,0:T(8,128)S(1)} %bitcast.79, ...), kind=kLoop, calls=%fused_computation.31.clone.1 | loop fusion | flops 16240640 | bytes 196608 | tf_op jit(solution)/shard_map/while/body/reduce_sum | solution.py:25
  87.5 1.8 scatter_fusion
  89.9 0.7 gather_fusion
  91.2 1.8 gather_fusion.4
  93.1 0.7 gather_fusion.1
  95.7 4.7 %fusion.43 = (f32[32,128]{1,0:T(8,128)S(1)}, f32[32,128]{1,0:T(8,128)S(1)}, f32[32,128]{1,0:T(8,128)S(1)}) fusion(f32[32,128]{1,0:T(8,128)} %bitcast.81, f32[32,128]{1,0:T(8,128)S(1)} %bitcast.84, f32[32,128]{1,0:T(8,128)S(1)} %bitcast.78, f32[32,128]{1,0:T(8,128)S(1)} %bitcast.85, f32[32,128]{1,0:T(8,128)S(1)} %bitcast.79, ...), kind=kLoop, calls=%fused_computation.31.clone.1 | loop fusion | flops 16240640 | bytes 196608 | tf_op jit(solution)/shard_map/while/body/reduce_sum | solution.py:25
  101.2 1.8 scatter_fusion
  103.6 0.7 gather_fusion
  104.9 1.8 gather_fusion.4
  106.8 0.7 gather_fusion.1
  109.4 4.7 %fusion.43 = (f32[32,128]{1,0:T(8,128)S(1)}, f32[32,128]{1,0:T(8,128)S(1)}, f32[32,128]{1,0:T(8,128)S(1)}) fusion(f32[32,128]{1,0:T(8,128)} %bitcast.81, f32[32,128]{1,0:T(8,128)S(1)} %bitcast.84, f32[32,128]{1,0:T(8,128)S(1)} %bitcast.78, f32[32,128]{1,0:T(8,128)S(1)} %bitcast.85, f32[32,128]{1,0:T(8,128)S(1)} %bitcast.79, ...), kind=kLoop, calls=%fused_computation.31.clone.1 | loop fusion | flops 16240640 | bytes 196608 | tf_op jit(solution)/shard_map/while/body/reduce_sum | solution.py:25
  114.9 1.8 scatter_fusion
  117.3 0.7 gather_fusion
  118.6 1.8 gather_fusion.4
  120.5 0.7 gather_fusion.1
  123.1 4.7 %fusion.43 = (f32[32,128]{1,0:T(8,128)S(1)}, f32[32,128]{1,0:T(8,128)S(1)}, f32[32,128]{1,0:T(8,128)S(1)}) fusion(f32[32,128]{1,0:T(8,128)} %bitcast.81, f32[32,128]{1,0:T(8,128)S(1)} %bitcast.84, f32[32,128]{1,0:T(8,128)S(1)} %bitcast.78, f32[32,128]{1,0:T(8,128)S(1)} %bitcast.85, f32[32,128]{1,0:T(8,128)S(1)} %bitcast.79, ...), kind=kLoop, calls=%fused_computation.31.clone.1 | loop fusion | flops 16240640 | bytes 196608 | tf_op jit(solution)/shard_map/while/body/reduce_sum | solution.py:25
  128.6 1.8 scatter_fusion
  130.9 0.7 gather_fusion
  132.3 1.8 gather_fusion.4
  134.1 0.7 gather_fusion.1
  136.8 4.7 %fusion.43 = (f32[32,128]{1,0:T(8,128)S(1)}, f32[32,128]{1,0:T(8,128)S(1)}, f32[32,128]{1,0:T(8,128)S(1)}) fusion(f32[32,128]{1,0:T(8,128)} %bitcast.81, f32[32,128]{1,0:T(8,128)S(1)} %bitcast.84, f32[32,128]{1,0:T(8,128)S(1)} %bitcast.78, f32[32,128]{1,0:T(8,128)S(1)} %bitcast.85, f32[32,128]{1,0:T(8,128)S(1)} %bitcast.79, ...), kind=kLoop, calls=%fused_computation.31.clone.1 | loop fusion | flops 16240640 | bytes 196608 | tf_op jit(solution)/shard_map/while/body/reduce_sum | solution.py:25
  142.2 1.8 scatter_fusion
  145.9 1.8 gather_fusion.4
  150.4 4.7 %fusion.43 = (f32[32,128]{1,0:T(8,128)S(1)}, f32[32,128]{1,0:T(8,128)S(1)}, f32[32,128]{1,0:T(8,128)S(1)}) fusion(f32[32,128]{1,0:T(8,128)} %bitcast.81, f32[32,128]{1,0:T(8,128)S(1)} %bitcast.84, f32[32,128]{1,0:T(8,128)S(1)} %bitcast.78, f32[32,128]{1,0:T(8,128)S(1)} %bitcast.85, f32[32,128]{1,0:T(8,128)S(1)} %bitcast.79, ...), kind=kLoop, calls=%fused_computation.31.clone.1 | loop fusion | flops 16240640 | bytes 196608 | tf_op jit(solution)/shard_map/while/body/reduce_sum | solution.py:25
  155.9 1.8 scatter_fusion
  157.8 1.0 copy-done.2
  158.8 3.2 sort.35
  162.1 1.4 gather_fusion.5
  165.6 168.4 %all-reduce.3.cloned.1.call-done = f32[512,3,128]{2,1,0:T(4,128)} async-done(((f32[512,3,128]{2,1,0:T(4,128)}), f32[512,3,128]{2,1,0:T(4,128)}) %all-reduce.3.cloned.1.call-update) | async-done | bytes 786448
  334.0 1.0 constant_dynamic-slice_fusion
  335.0 0.9 broadcast_in_dim.16
  335.9 12.5 %scatter_fusion.1 = f32[256,3,128]{2,1,0:T(4,128)} fusion(f32[256,3,128]{2,1,0:T(4,128)} %broadcast_in_dim.16, s32[128]{0:T(128)S(1)} %fusion.25, f32[128,3,128]{2,1,0:T(4,128)S(1)} %constant_dynamic-slice_fusion), kind=kCustom, calls=%fused_computation.14 | custom fusion | bytes 590336 | tf_op jit(solution)/shard_map/scatter | solution.py:102
  348.3 6.5 %all-to-all-start = ((f32[256,3,128]{2,1,0:T(4,128)}), f32[256,3,128]{2,1,0:T(4,128)S(1)}, u32[]{:S(2)}, u32[]{:S(2)}) async-start(f32[256,3,128]{2,1,0:T(4,128)} %scatter_fusion.1), calls=%async_computation | async-start | bytes 1048576 | tf_op jit(solution)/shard_map/all_to_all | solution.py:103
  355.9 12.5 %all-to-all-done = f32[256,3,128]{2,1,0:T(4,128)S(1)} async-done(((f32[256,3,128]{2,1,0:T(4,128)}), f32[256,3,128]{2,1,0:T(4,128)S(1)}, u32[]{:S(2)}, u32[]{:S(2)}) %all-to-all-start) | async-done | bytes 393248 | tf_op jit(solution)/shard_map/all_to_all | solution.py:103
  368.5 0.7 gather_fusion.10
  (141 shorter events, 28.5 us)
Async XLA Ops:
  6.5 63.4 %copy-start = (s32[1,512]{1,0:T(1,128)S(1)}, s32[1,512]{1,0:T(1,128)}, u32[]{:S(2)}) copy-start(s32[1,512]{1,0:T(1,128)} %param.15) | copy-start | bytes 6148
  6.5 327.5 %all-reduce.3.cloned.1.call-start = ((), (), s32[]{:S(2)}) async-start(), calls=%async_computation.1 | async-start | bytes 2097152
  11.7 5.4 %copy-start.3 = (f32[128,3,128]{2,0,1:T(8,128)S(1)}, f32[128,3,128]{2,0,1:T(8,128)}, u32[]{:S(2)}) copy-start(f32[128,3,128]{2,0,1:T(8,128)} %param.11) | copy-start | bytes 589828
  15.2 27.6 %copy-start.6 = (s32[256,8]{0,1:T(8,128)S(1)}, s32[256,8]{0,1:T(8,128)}, u32[]{:S(2)}) copy-start(s32[256,8]{0,1:T(8,128)} %param.18) | copy-start | bytes 24580
  17.1 26.0 %copy-start.7 = (s32[256,8]{0,1:T(8,128)S(1)}, s32[256,8]{0,1:T(8,128)}, u32[]{:S(2)}) copy-start(s32[256,8]{0,1:T(8,128)} %param.17) | copy-start | bytes 24580
  25.8 27.4 %copy-start.5 = (f32[128,128]{1,0:T(8,128)S(1)}, f32[128,128]{1,0:T(8,128)}, u32[]{:S(2)}) copy-start(f32[128,128]{1,0:T(8,128)} %param.13) | copy-start | bytes 196612
  25.8 27.5 %copy-start.4 = (f32[128,3,128]{2,0,1:T(8,128)S(1)}, f32[128,3,128]{2,0,1:T(8,128)}, u32[]{:S(2)}) copy-start(f32[128,3,128]{2,0,1:T(8,128)} %param.12) | copy-start | bytes 589828
  157.7 1.0 copy-start.2
  157.8 1.1 copy-start.1
  157.8 6.4 %copy-start.8 = (u32[32]{0:T(128)S(1)}, u32[32]{0:T(128)}, u32[]{:S(2)}) copy-start(u32[32]{0:T(128)} %constant.101) | copy-start | bytes 388
  348.3 20.1 %all-to-all-start = ((f32[256,3,128]{2,1,0:T(4,128)}), f32[256,3,128]{2,1,0:T(4,128)S(1)}, u32[]{:S(2)}, u32[]{:S(2)}) async-start(f32[256,3,128]{2,1,0:T(4,128)} %scatter_fusion.1), calls=%async_computation | async-start | bytes 1048576 | tf_op jit(solution)/shard_map/all_to_all | solution.py:103
Sparse Core Ops, SparseCore 0:
  158.9 175.0 all-reduce.2
where the time goes:
time: 381 us; the launch traced here: 377 us
  waiting for transfers between devices  181 us (48%)
  local copies, waits for them, and re-layouts  70.9 us (19%)
  other arithmetic  56.6 us (15%)
  blocking collectives  41.7 us (11%)
  between operations  16.2 us (4%)
  starting transfers between devices  6.54 us (2%)
  loops' own time  3.85 us (1%)
    unnamed x2, waiting for transfers between devices  168 us
    reduce_sum x6, other arithmetic, stokeslet(): speed_x = jnp.sum(isotropic * force_x + project * delta_x, axis=2)  28.2 us
    all_gather x1, blocking collectives, per_device(): lax.all_gather(positions, 'row', axis=0, tiled=True)  17 us
    all_gather x1, blocking collectives, per_device(): lax.all_gather(forces, 'row', axis=0, tiled=True)  16 us
    all_to_all x1, waiting for transfers between devices, per_device(): lax.all_to_all(outgoing, ('row', 'col'), split_axis=0, concat_axis=0, til...  12.5 us
    scatter x1, local copies, waits for them, and re-layouts, per_device(): outgoing = outgoing.at[home_owner * capacity + send_rank].set(home_speed)  12.5 us
    gather x6, local copies, waits for them, and re-layouts, accumulate(): targets[target_ids]  11 us
    scatter-add x6, other arithmetic, accumulate(): return totals.at[offsets].add(speeds)  10.7 us
  transfers between devices with their start and end apart: 2, of which 2 were waited for; matrix products, arithmetic and copies ran while one was open for 2% of the time, Pallas kernels for 0%

commit v1 on v0

v1 whole, which is shorter than its diff:
```python
import functools
import math

import jax
import jax.numpy as jnp
from jax import lax
from jax.experimental import pallas as pl
from jax.experimental.pallas import tpu as pltpu
from jax.sharding import PartitionSpec as P

regular_sq = 0.0025
stokes_scale = 1.0 / (8.0 * math.pi)
MESH = pl.DeviceIdType.MESH
VMEM = pl.BlockSpec(memory_space=pltpu.VMEM)
SMEM = pl.BlockSpec(memory_space=pltpu.SMEM)


def gather_kernel(nrow, ncol, pos_ref, nrm_ref, curv_ref, cnt_ref, t_ref, s_ref, tsend, trecv, ssend, srecv):
    row, col = lax.axis_index("row"), lax.axis_index("col")
    local = pos_ref.shape[0]
    barrier = pltpu.get_barrier_semaphore()
    for d in range(1, nrow):
        pl.semaphore_signal(barrier, inc=1, device_id={"row": lax.rem(row + d, nrow)}, device_id_type=MESH)
    for d in range(1, ncol):
        pl.semaphore_signal(barrier, inc=1, device_id={"col": lax.rem(col + d, ncol)}, device_id_type=MESH)
    tmine = pl.ds(pl.multiple_of(col * local, local), local)
    smine = pl.ds(pl.multiple_of(row * local, local), local)
    live = lax.broadcasted_iota(jnp.int32, curv_ref.shape, 1) < cnt_ref[...]
    scale = jnp.where(live, curv_ref[...], 0.0)
    for k in range(3):
        coord = pos_ref[:, k, :]
        t_ref[k, tmine, :] = coord
        s_ref[k, smine, :] = coord
        s_ref[3 + k, smine, :] = scale * nrm_ref[:, k, :]
    pl.semaphore_wait(barrier, nrow + ncol - 2)
    copies = []
    for d in range(1, nrow):
        copies.append(pltpu.make_async_remote_copy(
            src_ref=s_ref.at[:, smine, :], dst_ref=s_ref.at[:, smine, :],
            send_sem=ssend.at[d - 1], recv_sem=srecv.at[d - 1],
            device_id={"row": lax.rem(row + d, nrow)}, device_id_type=MESH))
    for d in range(1, ncol):
        copies.append(pltpu.make_async_remote_copy(
            src_ref=t_ref.at[:, tmine, :], dst_ref=t_ref.at[:, tmine, :],
            send_sem=tsend.at[d - 1], recv_sem=trecv.at[d - 1],
            device_id={"col": lax.rem(col + d, ncol)}, device_id_type=MESH))
    for copy in copies:
        copy.start()
    for copy in copies:
        copy.wait()


def pair_kernel(tgt_ref, src_ref, count_ref, t_ref, s_ref, v_ref, sc_ref):
    v_ref[...] = jnp.zeros_like(v_ref)
    for k in range(6):
        sc_ref[:, k, :] = s_ref[k]
    step = 32

    def one(e, carry):
        t, s = tgt_ref[0, e], src_ref[0, e]
        tx, ty, tz = (t_ref[k, pl.ds(t, 1), :] for k in range(3))
        turned = sc_ref[s].T
        total = [jnp.zeros((8, 128), jnp.float32) for _ in range(3)]
        for i in range(128 // step):
            part = turned[i * step:(i + 1) * step]
            dx, dy, dz = tx - part[:, 0:1], ty - part[:, 1:2], tz - part[:, 2:3]
            fx, fy, fz = part[:, 3:4], part[:, 4:5], part[:, 5:6]
            inv = lax.rsqrt(dx * dx + dy * dy + dz * dz + regular_sq)
            weight = inv * inv * inv
            iso = inv + regular_sq * weight
            proj = (dx * fx + dy * fy + dz * fz) * weight
            for k, (f, w) in enumerate(((fx, dx), (fy, dy), (fz, dz))):
                total[k] += (iso * f + proj * w).reshape(step // 8, 8, 128).sum(axis=0)
        for k in range(3):
            v_ref[k, pl.ds(t, 1), :] += stokes_scale * jnp.sum(total[k], axis=0, keepdims=True)
        return carry

    lax.fori_loop(0, count_ref[0], one, 0)


def home_kernel(nrow, ncol, cap, pack_ref, unpack_ref, cnt_ref, v_ref, out_ref, got, home, outg, arr, vsend, vrecv, asend, arecv):
    row, col = lax.axis_index("row"), lax.axis_index("col")
    local = out_ref.shape[0]
    devs = nrow * ncol
    me = row * ncol + col
    barrier = pltpu.get_barrier_semaphore()

    def peer(d):
        p = lax.rem(me + d, devs)
        return {"row": p // ncol, "col": lax.rem(p, ncol)}

    for d in range(1, devs):
        pl.semaphore_signal(barrier, inc=1, device_id=peer(d), device_id_type=MESH)
    pl.semaphore_wait(barrier, devs - 1)
    copies = []
    for d in range(1, ncol):
        to = lax.rem(col + d, ncol)
        copies.append(pltpu.make_async_remote_copy(
            src_ref=v_ref.at[:, pl.ds(pl.multiple_of(to * local, local), local), :],
            dst_ref=got.at[d - 1], send_sem=vsend.at[d - 1], recv_sem=vrecv.at[d - 1],
            device_id={"col": to}, device_id_type=MESH))
    for copy in copies:
        copy.start()
    for copy in copies:
        copy.wait()
    for k in range(3):
        mine = v_ref[k, pl.ds(pl.multiple_of(col * local, local), local), :]
        for d in range(1, ncol):
            mine = mine + got[d - 1, k]
        home[:, k, :] = mine

    unroll = 8

    def pack(i, carry):
        for u in range(unroll):
            slot = i * unroll + u
            outg[slot] = home[pack_ref[slot], 0:3, :]
        return carry

    lax.fori_loop(0, devs * cap // unroll, pack, 0)
    copies = []
    own = pl.ds(me * cap, cap)
    for d in range(1, devs):
        p = lax.rem(me + d, devs)
        copies.append(pltpu.make_async_remote_copy(
            src_ref=outg.at[pl.ds(p * cap, cap)], dst_ref=arr.at[own],
            send_sem=asend.at[d - 1], recv_sem=arecv.at[d - 1],
            device_id=peer(d), device_id_type=MESH))
    for copy in copies:
        copy.start()
    arr[own] = outg[own]
    for copy in copies:
        copy.wait()
    slots = lax.broadcasted_iota(jnp.int32, (3, 128), 1)

    def unpack(i, carry):
        for u in range(unroll):
            n = i * unroll + u
            out_ref[n] = jnp.where(slots < cnt_ref[n], arr[unpack_ref[n]], 0.0)
        return carry

    lax.fori_loop(0, local // unroll, unpack, 0)


def per_device(positions, normals, curvature, pair_targets, pair_sources, pair_count, node_counts, drop_clusters, drop_owner):
    local, _, nodes = positions.shape
    nrow, ncol = lax.axis_size("row"), lax.axis_size("col")
    devs = nrow * ncol
    me = lax.axis_index("row") * ncol + lax.axis_index("col")
    cap = max(2, 2 * local // devs)
    per_drop = drop_clusters.shape[1]
    drops = drop_owner.shape[0]
    here = local // per_drop
    ints = jnp.int32

    flat_clusters = drop_clusters.reshape(-1)
    flat_counts = node_counts.reshape(-1)
    flat_owner = jnp.broadcast_to(drop_owner[:, None], (drops, per_drop)).reshape(-1)
    order = jnp.arange(local, dtype=ints)
    hit = (me * local + order)[:, None] == flat_clusters[None, :]
    home_counts = jnp.sum(jnp.where(hit, flat_counts[None, :], 0), axis=1, dtype=ints)
    home_owner = jnp.sum(jnp.where(hit, flat_owner[None, :], 0), axis=1, dtype=ints)
    rank = jnp.sum((home_owner[None, :] == home_owner[:, None]) & (order[None, :] < order[:, None]), axis=1, dtype=ints)
    slot_of = home_owner * cap + rank
    all_slots = jnp.arange(devs * cap, dtype=ints)
    pack = jnp.sum(jnp.where(slot_of[None, :] == all_slots[:, None], order[None, :], 0), axis=1, dtype=ints)

    drop_ids = jnp.arange(drops, dtype=ints)
    mine = drop_owner == me
    place = jnp.sum(mine[None, :] & (drop_ids[None, :] < drop_ids[:, None]), axis=1, dtype=ints)
    chosen = mine[None, :] & (place[None, :] == jnp.arange(here, dtype=ints)[:, None])
    owned_clusters = jnp.sum(jnp.where(chosen[:, :, None], drop_clusters[None], 0), axis=1, dtype=ints).reshape(-1)
    owned_counts = jnp.sum(jnp.where(chosen[:, :, None], node_counts[None], 0), axis=1, dtype=ints).reshape(-1)
    anchor = owned_clusters // local
    before = (anchor[None, :] == anchor[:, None]) & (owned_clusters[None, :] < owned_clusters[:, None])
    unpack = anchor * cap + jnp.sum(before, axis=1, dtype=ints)

    dma = pltpu.SemaphoreType.DMA
    f32 = jnp.float32
    targets, sources = pl.pallas_call(
        functools.partial(gather_kernel, nrow, ncol),
        out_shape=(jax.ShapeDtypeStruct((3, ncol * local, nodes), f32), jax.ShapeDtypeStruct((6, nrow * local, nodes), f32)),
        in_specs=[VMEM] * 4, out_specs=(VMEM, VMEM),
        scratch_shapes=[dma((ncol - 1,)), dma((ncol - 1,)), dma((nrow - 1,)), dma((nrow - 1,))],
        compiler_params=pltpu.CompilerParams(collective_id=0, has_side_effects=True, vmem_limit_bytes=56 << 20),
        name="gather_blocks",
    )(positions, normals, curvature, home_counts[:, None])
    speeds = pl.pallas_call(
        pair_kernel,
        out_shape=jax.ShapeDtypeStruct((3, ncol * local, nodes), f32),
        in_specs=[SMEM] * 3 + [VMEM] * 2, out_specs=VMEM,
        scratch_shapes=[pltpu.VMEM((nrow * local, 8, nodes), f32)],
        compiler_params=pltpu.CompilerParams(vmem_limit_bytes=56 << 20),
        name="pairs",
    )(pair_targets, pair_sources, pair_count, targets, sources)
    return pl.pallas_call(
        functools.partial(home_kernel, nrow, ncol, cap),
        out_shape=jax.ShapeDtypeStruct((local, 3, nodes), f32),
        in_specs=[SMEM] * 3 + [VMEM], out_specs=VMEM,
        scratch_shapes=[
            pltpu.VMEM((ncol - 1, 3, local, nodes), f32), pltpu.VMEM((local, 8, nodes), f32),
            pltpu.VMEM((devs * cap, 3, nodes), f32), pltpu.VMEM((devs * cap, 3, nodes), f32),
            dma((ncol - 1,)), dma((ncol - 1,)), dma((devs - 1,)), dma((devs - 1,)),
        ],
        compiler_params=pltpu.CompilerParams(collective_id=1, has_side_effects=True, vmem_limit_bytes=56 << 20),
        name="to_owners",
    )(pack, unpack, owned_counts, speeds)


def solution(mesh):
    every = ("groups", "row", "col")
    in_specs = (
        P(every, None, None), P(every, None, None), P(every, None), P(every, None), P(every, None), P(every),
        P("groups", None), P("groups", None), P("groups"),
    )
    return jax.shard_map(per_device, mesh=mesh, in_specs=in_specs, out_specs=P(every, None, None), check_vma=False)
```

time: 381 us -> 247 us (0.65); the launches traced: 377 us -> 247 us
  Pallas kernels: 0 us -> 234 us
  waiting for transfers between devices: 181 us -> 0 us
  local copies, waits for them, and re-layouts: 70.9 us -> 8.5 us
  other arithmetic: 56.6 us -> 4.08 us
  blocking collectives: 41.7 us -> 0 us
  between operations: 16.2 us -> 0.78 us
  starting transfers between devices: 6.54 us -> 0 us
  loops' own time: 3.85 us -> 0 us
    pallas_call x0 -> x3, Pallas kernels: none -> 234 us  [the longest x1 132 us: per_device(): pl.pallas_call(functools.partial(home_kernel, nrow, ncol, cap), out_shape...]
    unnamed x2 -> x0, waiting for transfers between devices: 168 us -> none
    all_gather x3 -> x0, blocking collectives: 41.7 us -> none  [the longest x1 17 us: per_device(): lax.all_gather(positions, 'row', axis=0, tiled=True)]
    gather x37 -> x0, local copies, waits for them, and re-layouts: 38.2 us -> none  [the longest x6 11 us: accumulate(): targets[target_ids]]
    reduce_sum x9 -> x6, other arithmetic: 29.2 us -> 2.83 us  [the longest x1 1.33 us: per_device(): jnp.sum(jnp.where(chosen[:, :, None], node_counts[None], 0), axis=1, dtyp...]
    scatter x2 -> x0, local copies, waits for them, and re-layouts: 20.5 us -> none  [the longest x1 12.5 us: per_device(): outgoing = outgoing.at[home_owner * capacity + send_rank].set(home_speed)]
    all_to_all x1 -> x0, waiting for transfers between devices: 12.5 us -> none  [per_device(): lax.all_to_all(outgoing, ('row', 'col'), split_axis=0, concat_axis=0, til...]
    scatter-add x6 -> x0, other arithmetic: 10.7 us -> none  [accumulate(): return totals.at[offsets].add(speeds)]
  transfers between devices with their start and end apart: 2 -> 0, of which waited for: 2 -> 0; matrix products, arithmetic and copies ran while one was open for 2% -> 0% of each run, Pallas kernels for 0% -> 0%
where the time goes in v1:
time: 247 us
  Pallas kernels  234 us (95%)
  local copies, waits for them, and re-layouts  8.5 us (3%)
  other arithmetic  4.08 us (2%)
    pallas_call x1, Pallas kernels, per_device(): pl.pallas_call(functools.partial(home_kernel, nrow, ncol, cap), out_shape...  132 us
    pallas_call x1, Pallas kernels, per_device(): pl.pallas_call(pair_kernel, out_shape=jax.ShapeDtypeStruct((3, ncol * loc...  62.9 us
    pallas_call x1, Pallas kernels, per_device(): pl.pallas_call(functools.partial(gather_kernel, nrow, ncol), out_shape=(j...  39.5 us

profile of v1, /device:TPU:15, one launch (start us, length us, event | category | flops | bytes accessed | tf_op | source)
XLA Modules:
  0.0 247.4 jit_solution(12708906588610934828)
XLA Ops:
  0.0 0.0 copy-start
  0.7 0.7 broadcast_compare_fusion
  1.4 0.1 convert_reduce_fusion
  1.5 1.3 select_reduce_fusion
  2.9 0.7 reshape.113.cnt_ref
  3.5 0.1 reshape.112
  3.6 0.2 convert_reduce_fusion.1
  3.8 0.5 multiply_add_fusion.unpack_ref
  4.4 0.8 copy.25
  5.2 0.1 broadcast_in_dim.102
  5.3 0.8 copy.24
  6.1 0.1 eq.78
  6.2 0.8 broadcast_in_dim.92
  7.0 0.1 broadcast_in_dim.93
  7.1 0.3 fusion.1
  7.5 0.2 convert_reduce_fusion.2
  7.6 0.7 select_reduce_fusion.2.pack_ref
  8.3 0.7 copy.28.cnt_ref
  9.1 1.8 copy.26.pos_ref
  10.9 0.0 copy-done
  10.9 0.8 copy.27.nrm_ref
  11.7 39.5 %gather_blocks.1 = (f32[3,512,128]{2,1,0:T(8,128)}, f32[6,512,128]{2,1,0:T(8,128)}) custom-call(f32[128,3,128]{2,1,0:T(4,128)} %copy.26.pos_ref, f32[128,3,128]{2,1,0:T(4,128)} %copy.27.nrm_ref, f32[128,128]{1,0:T(8,128)} %curv_ref.1, s32[128,1]{1,0:T(8,128)} %copy.28.cnt_ref), custom_call_target="tpu_custom_call" | custom-call | tf_op jit(solution)/shard_map/gather_blocks/pallas_call | solution.py:180
  51.2 62.9 %pairs.1.v_ref = f32[3,512,128]{2,1,0:T(8,128)} custom-call(s32[1,512]{1,0:T(1,128)} %tgt_ref.1, s32[1,512]{1,0:T(1,128)} %src_ref.1, s32[1]{0:T(128)S(6)} %copy.30.count_ref, f32[3,512,128]{2,1,0:T(8,128)} %get-tuple-element.7.t_ref, f32[6,512,128]{2,1,0:T(8,128)} %get-tuple-element.8.s_ref), custom_call_target="tpu_custom_call" | custom-call | tf_op jit(solution)/shard_map/pairs/pallas_call | solution.py:188
  114.1 131.7 %to_owners.1 = f32[128,3,128]{2,1,0:T(4,128)} custom-call(s32[256]{0:T(256)} %select_reduce_fusion.2.pack_ref, s32[128]{0:T(128)} %multiply_add_fusion.unpack_ref, s32[128]{0:T(128)} %reshape.113.cnt_ref, f32[3,512,128]{2,1,0:T(8,128)} %pairs.1.v_ref), custom_call_target="tpu_custom_call" | custom-call | tf_op jit(solution)/shard_map/to_owners/pallas_call | solution.py:196
  245.7 1.6 copy.29
  (4 shorter events, 0.0 us)
Async XLA Ops:
  0.0 10.9 %copy-start = (f32[128,3,128]{2,0,1:T(8,128)S(1)}, f32[128,3,128]{2,0,1:T(8,128)}, u32[]{:S(2)}) copy-start(f32[128,3,128]{2,0,1:T(8,128)} %param.10) | copy-start | bytes 589828

commit v2 on v1

--- a/solution.py
+++ b/solution.py
@@ -15,33 +15,33 @@
 SMEM = pl.BlockSpec(memory_space=pltpu.SMEM)
 
 
+unroll = 4
+
+
 def gather_kernel(nrow, ncol, pos_ref, nrm_ref, curv_ref, cnt_ref, t_ref, s_ref, tsend, trecv, ssend, srecv):
     row, col = lax.axis_index("row"), lax.axis_index("col")
-    local = pos_ref.shape[0]
     barrier = pltpu.get_barrier_semaphore()
     for d in range(1, nrow):
         pl.semaphore_signal(barrier, inc=1, device_id={"row": lax.rem(row + d, nrow)}, device_id_type=MESH)
     for d in range(1, ncol):
         pl.semaphore_signal(barrier, inc=1, device_id={"col": lax.rem(col + d, ncol)}, device_id_type=MESH)
-    tmine = pl.ds(pl.multiple_of(col * local, local), local)
-    smine = pl.ds(pl.multiple_of(row * local, local), local)
     live = lax.broadcasted_iota(jnp.int32, curv_ref.shape, 1) < cnt_ref[...]
     scale = jnp.where(live, curv_ref[...], 0.0)
     for k in range(3):
         coord = pos_ref[:, k, :]
-        t_ref[k, tmine, :] = coord
-        s_ref[k, smine, :] = coord
-        s_ref[3 + k, smine, :] = scale * nrm_ref[:, k, :]
+        t_ref[col, k] = coord
+        s_ref[row, k] = coord
+        s_ref[row, 3 + k] = scale * nrm_ref[:, k, :]
     pl.semaphore_wait(barrier, nrow + ncol - 2)
     copies = []
     for d in range(1, nrow):
         copies.append(pltpu.make_async_remote_copy(
-            src_ref=s_ref.at[:, smine, :], dst_ref=s_ref.at[:, smine, :],
+            src_ref=s_ref.at[row], dst_ref=s_ref.at[row],
             send_sem=ssend.at[d - 1], recv_sem=srecv.at[d - 1],
             device_id={"row": lax.rem(row + d, nrow)}, device_id_type=MESH))
     for d in range(1, ncol):
         copies.append(pltpu.make_async_remote_copy(
-            src_ref=t_ref.at[:, tmine, :], dst_ref=t_ref.at[:, tmine, :],
+            src_ref=t_ref.at[col], dst_ref=t_ref.at[col],
             send_sem=tsend.at[d - 1], recv_sem=trecv.at[d - 1],
             device_id={"col": lax.rem(col + d, ncol)}, device_id_type=MESH))
     for copy in copies:
@@ -50,32 +50,95 @@
         copy.wait()
 
 
-def pair_kernel(tgt_ref, src_ref, count_ref, t_ref, s_ref, v_ref, sc_ref):
+def split3(x):
+    high = x.astype(jnp.bfloat16).astype(jnp.float32)
+    rest = x - high
+    middle = rest.astype(jnp.bfloat16).astype(jnp.float32)
+    return high, middle, rest - middle
+
+
+def split2(x):
+    high = x.astype(jnp.bfloat16)
+    return high, (x - high.astype(jnp.float32)).astype(jnp.bfloat16)
+
+
+def pair_kernel(tgt_ref, src_ref, count_ref, t_ref, s_ref, v_ref, tc_ref, sc_ref):
+    ncol, _, local, _ = t_ref.shape
+    nrow = s_ref.shape[0]
+    slots = tgt_ref.shape[1]
+    f32 = jnp.float32
     v_ref[...] = jnp.zeros_like(v_ref)
-    for k in range(6):
-        sc_ref[:, k, :] = s_ref[k]
-    step = 32
-
-    def one(e, carry):
-        t, s = tgt_ref[0, e], src_ref[0, e]
-        tx, ty, tz = (t_ref[k, pl.ds(t, 1), :] for k in range(3))
-        turned = sc_ref[s].T
-        total = [jnp.zeros((8, 128), jnp.float32) for _ in range(3)]
-        for i in range(128 // step):
-            part = turned[i * step:(i + 1) * step]
-            dx, dy, dz = tx - part[:, 0:1], ty - part[:, 1:2], tz - part[:, 2:3]
-            fx, fy, fz = part[:, 3:4], part[:, 4:5], part[:, 5:6]
-            inv = lax.rsqrt(dx * dx + dy * dy + dz * dz + regular_sq)
+
+    def targets(c, carry):
+        rows = pl.ds(pl.multiple_of(c * local, local), local)
+        square = jnp.full((local, 128), regular_sq, f32)
+        for k in range(3):
+            coord = t_ref[c, k]
+            centre = jnp.mean(coord, axis=1, keepdims=True)
+            coord = coord - centre
+            square = square + coord * coord
+            tc_ref[rows, k, :] = coord
+            tc_ref[rows, 5 + k, :] = jnp.broadcast_to(centre, coord.shape)
+        tc_ref[rows, 3, :] = square
+        tc_ref[rows, 4, :] = jnp.ones((local, 128), f32)
+        return carry
+
+    lax.fori_loop(0, ncol, targets, 0)
+
+    def sources(r, carry):
+        rows = pl.ds(pl.multiple_of(r * local, local), local)
+        for k in range(6):
+            sc_ref[rows, k, :] = s_ref[r, k]
+        return carry
+
+    lax.fori_loop(0, nrow, sources, 0)
+    count = count_ref[0]
+    ones = jnp.ones((1, 128), f32)
+    none = jnp.zeros((3, 128), f32)
+
+    def many(block, carry):
+        made = []
+        for u in range(unroll):
+            e = block * unroll + u
+            active = e < count
+            e = jnp.minimum(e, slots - 1)
+            t, s = tgt_ref[0, e], src_ref[0, e]
+            near = tc_ref[t]
+            far = sc_ref[s]
+            shifted = far[0:3] - near[5:8]
+            force = jnp.where(active, far[3:6], 0.0)
+            square = jnp.sum(shifted * shifted, axis=0, keepdims=True)
+            along = jnp.sum(shifted * force, axis=0, keepdims=True)
+            a_hi, a_mid, a_lo = split3(jnp.concatenate([near[0:5], none], axis=0))
+            b_hi, b_mid, b_lo = split3(jnp.concatenate([-2.0 * shifted, ones, square, none], axis=0))
+            c_hi, c_mid, c_lo = split3(jnp.concatenate([force, 0.0 * ones, -along, none], axis=0))
+            right = jnp.concatenate([a_hi, a_mid, a_lo, a_hi, a_mid, a_hi], axis=0).astype(jnp.bfloat16)
+            left = jnp.concatenate([
+                jnp.concatenate([b_hi, b_hi, b_hi, b_mid, b_mid, b_lo], axis=0),
+                jnp.concatenate([c_hi, c_hi, c_hi, c_mid, c_mid, c_lo], axis=0)], axis=1).astype(jnp.bfloat16)
+            both = lax.dot_general(left, right, (((0,), (0,)), ((), ())), preferred_element_type=f32)
+            gathered = jnp.concatenate([force, shifted, ones, ones], axis=0)
+            g_hi = gathered.astype(jnp.bfloat16).astype(f32)
+            g = jnp.concatenate([g_hi, gathered - g_hi], axis=0).astype(jnp.bfloat16)
+            made.append((t, near, both, g))
+        results = []
+        for t, near, both, g in made:
+            inv = lax.rsqrt(both[0:128])
             weight = inv * inv * inv
-            iso = inv + regular_sq * weight
-            proj = (dx * fx + dy * fy + dz * fz) * weight
-            for k, (f, w) in enumerate(((fx, dx), (fy, dy), (fz, dz))):
-                total[k] += (iso * f + proj * w).reshape(step // 8, 8, 128).sum(axis=0)
-        for k in range(3):
-            v_ref[k, pl.ds(t, 1), :] += stokes_scale * jnp.sum(total[k], axis=0, keepdims=True)
-        return carry
-
-    lax.fori_loop(0, count_ref[0], one, 0)
+            iso_hi, iso_lo = split2(inv + regular_sq * weight)
+            pro_hi, pro_lo = split2(both[128:256] * weight)
+            m = jnp.concatenate([
+                jnp.concatenate([iso_hi, pro_hi], axis=1), jnp.concatenate([iso_lo, pro_lo], axis=1)], axis=0)
+            out = jnp.dot(jnp.concatenate([g, g], axis=1), m, preferred_element_type=f32)
+            out = out[0:8] + out[8:16]
+            results.append((t, stokes_scale * (out[0:3, 0:128] + near[0:3] * out[6:7, 128:256] - out[3:6, 128:256])))
+        for t, speed in results:
+            c, i = t // local, lax.rem(t, local)
+            for k in range(3):
+                v_ref[c, k, pl.ds(i, 1), :] += speed[k:k + 1]
+        return carry
+
+    lax.fori_loop(0, (count + unroll - 1) // unroll, many, 0)
 
 
 def home_kernel(nrow, ncol, cap, pack_ref, unpack_ref, cnt_ref, v_ref, out_ref, got, home, outg, arr, vsend, vrecv, asend, arecv):
@@ -96,50 +159,49 @@
     for d in range(1, ncol):
         to = lax.rem(col + d, ncol)
         copies.append(pltpu.make_async_remote_copy(
-            src_ref=v_ref.at[:, pl.ds(pl.multiple_of(to * local, local), local), :],
-            dst_ref=got.at[d - 1], send_sem=vsend.at[d - 1], recv_sem=vrecv.at[d - 1],
+            src_ref=v_ref.at[to], dst_ref=got.at[d - 1], send_sem=vsend.at[d - 1], recv_sem=vrecv.at[d - 1],
             device_id={"col": to}, device_id_type=MESH))
     for copy in copies:
         copy.start()
     for copy in copies:
         copy.wait()
     for k in range(3):
-        mine = v_ref[k, pl.ds(pl.multiple_of(col * local, local), local), :]
+        mine = v_ref[col, k]
         for d in range(1, ncol):
             mine = mine + got[d - 1, k]
         home[:, k, :] = mine
 
-    unroll = 8
-
-    def pack(i, carry):
-        for u in range(unroll):
-            slot = i * unroll + u
-            outg[slot] = home[pack_ref[slot], 0:3, :]
-        return carry
-
-    lax.fori_loop(0, devs * cap // unroll, pack, 0)
+    def pack(p, carry):
+        for j in range(cap):
+            one = home[pack_ref[p * cap + j]]
+            for k in range(3):
+                outg[p, k, j:j + 1, :] = one[k:k + 1]
+        return carry
+
+    lax.fori_loop(0, devs, pack, 0)
     copies = []
-    own = pl.ds(me * cap, cap)
     for d in range(1, devs):
-        p = lax.rem(me + d, devs)
-        copies.append(pltpu.make_async_remote_copy(
-            src_ref=outg.at[pl.ds(p * cap, cap)], dst_ref=arr.at[own],
+        copies.append(pltpu.make_async_remote_copy(
+            src_ref=outg.at[lax.rem(me + d, devs)], dst_ref=arr.at[me],
             send_sem=asend.at[d - 1], recv_sem=arecv.at[d - 1],
             device_id=peer(d), device_id_type=MESH))
     for copy in copies:
         copy.start()
-    arr[own] = outg[own]
+    arr[me] = outg[me]
     for copy in copies:
         copy.wait()
-    slots = lax.broadcasted_iota(jnp.int32, (3, 128), 1)
+    slots = lax.broadcasted_iota(jnp.int32, (1, 128), 1)
 
     def unpack(i, carry):
-        for u in range(unroll):
-            n = i * unroll + u
-            out_ref[n] = jnp.where(slots < cnt_ref[n], arr[unpack_ref[n]], 0.0)
-        return carry
-
-    lax.fori_loop(0, local // unroll, unpack, 0)
+        for u in range(8):
+            n = i * 8 + u
+            at = unpack_ref[n]
+            live = slots < cnt_ref[n]
+            for k in range(3):
+                out_ref[n, k:k + 1, :] = jnp.where(live, arr[at // cap, k, pl.ds(lax.rem(at, cap), 1), :], 0.0)
+        return carry
+
+    lax.fori_loop(0, local // 8, unpack, 0)
 
 
 def per_device(positions, normals, curvature, pair_targets, pair_sources, pair_count, node_counts, drop_clusters, drop_owner):
@@ -179,7 +241,7 @@
     f32 = jnp.float32
     targets, sources = pl.pallas_call(
         functools.partial(gather_kernel, nrow, ncol),
-        out_shape=(jax.ShapeDtypeStruct((3, ncol * local, nodes), f32), jax.ShapeDtypeStruct((6, nrow * local, nodes), f32)),
+        out_shape=(jax.ShapeDtypeStruct((ncol, 3, local, nodes), f32), jax.ShapeDtypeStruct((nrow, 6, local, nodes), f32)),
         in_specs=[VMEM] * 4, out_specs=(VMEM, VMEM),
         scratch_shapes=[dma((ncol - 1,)), dma((ncol - 1,)), dma((nrow - 1,)), dma((nrow - 1,))],
         compiler_params=pltpu.CompilerParams(collective_id=0, has_side_effects=True, vmem_limit_bytes=56 << 20),
@@ -187,9 +249,9 @@
     )(positions, normals, curvature, home_counts[:, None])
     speeds = pl.pallas_call(
         pair_kernel,
-        out_shape=jax.ShapeDtypeStruct((3, ncol * local, nodes), f32),
+        out_shape=jax.ShapeDtypeStruct((ncol, 3, local, nodes), f32),
         in_specs=[SMEM] * 3 + [VMEM] * 2, out_specs=VMEM,
-        scratch_shapes=[pltpu.VMEM((nrow * local, 8, nodes), f32)],
+        scratch_shapes=[pltpu.VMEM((ncol * local, 8, nodes), f32), pltpu.VMEM((nrow * local, 8, nodes), f32)],
         compiler_params=pltpu.CompilerParams(vmem_limit_bytes=56 << 20),
         name="pairs",
     )(pair_targets, pair_sources, pair_count, targets, sources)
@@ -199,7 +261,7 @@
         in_specs=[SMEM] * 3 + [VMEM], out_specs=VMEM,
         scratch_shapes=[
             pltpu.VMEM((ncol - 1, 3, local, nodes), f32), pltpu.VMEM((local, 8, nodes), f32),
-            pltpu.VMEM((devs * cap, 3, nodes), f32), pltpu.VMEM((devs * cap, 3, nodes), f32),
+            pltpu.VMEM((devs, 3, cap, nodes), f32), pltpu.VMEM((devs, 3, cap, nodes), f32),
             dma((ncol - 1,)), dma((ncol - 1,)), dma((devs - 1,)), dma((devs - 1,)),
         ],
         compiler_params=pltpu.CompilerParams(collective_id=1, has_side_effects=True, vmem_limit_bytes=56 << 20),

time: 247 us -> 142 us (0.57)
  Pallas kernels: 234 us -> 127 us
    pallas_call x1, Pallas kernels: 132 us -> 70.2 us  [per_device(): pl.pallas_call(functools.partial(home_kernel, nrow, ncol, cap), out_shape...]
    pallas_call x1, Pallas kernels: 62.9 us -> 17 us  [per_device(): pl.pallas_call(pair_kernel, out_shape=jax.ShapeDtypeStruct((ncol, 3, loca...]
where the time goes in v2:
time: 142 us; the launch traced here: 140 us
  Pallas kernels  127 us (89%)
  local copies, waits for them, and re-layouts  8.5 us (6%)
  other arithmetic  4.08 us (3%)
    pallas_call x1, Pallas kernels, per_device(): pl.pallas_call(functools.partial(home_kernel, nrow, ncol, cap), out_shape...  70.2 us
    pallas_call x1, Pallas kernels, per_device(): pl.pallas_call(functools.partial(gather_kernel, nrow, ncol), out_shape=(j...  39.5 us
    pallas_call x1, Pallas kernels, per_device(): pl.pallas_call(pair_kernel, out_shape=jax.ShapeDtypeStruct((ncol, 3, loca...  17 us
    unnamed x6, local copies, waits for them, and re-layouts  4.25 us

profile of v2, /device:TPU:15, one launch (start us, length us, event | category | flops | bytes accessed | tf_op | source)
XLA Modules:
  0.0 140.0 jit_solution(12978464288407355436)
XLA Ops:
  0.0 0.0 copy-start
  0.7 0.7 broadcast_compare_fusion
  1.4 0.1 convert_reduce_fusion
  1.5 1.3 select_reduce_fusion
  2.9 0.7 reshape.113.cnt_ref
  3.5 0.1 reshape.112
  3.6 0.2 convert_reduce_fusion.1
  3.8 0.5 multiply_add_fusion.unpack_ref
  4.4 0.8 copy.25
  5.2 0.1 broadcast_in_dim.102
  5.3 0.8 copy.24
  6.1 0.1 eq.78
  6.2 0.8 broadcast_in_dim.92
  7.0 0.1 broadcast_in_dim.93
  7.1 0.3 fusion.1
  7.5 0.2 convert_reduce_fusion.2
  7.6 0.7 select_reduce_fusion.2.pack_ref
  8.3 0.7 copy.28.cnt_ref
  9.1 1.8 %copy.26.pos_ref = f32[128,3,128]{2,1,0:T(4,128)} copy(f32[128,3,128]{2,0,1:T(8,128)} %param.9) | data formatting | bytes 393216 | tf_op args[0]
  10.9 0.0 copy-done
  10.9 0.8 copy.27.nrm_ref
  11.7 39.5 %gather_blocks.1 = (f32[4,3,128,128]{3,2,1,0:T(8,128)}, f32[4,6,128,128]{3,2,1,0:T(8,128)}) custom-call(f32[128,3,128]{2,1,0:T(4,128)} %copy.26.pos_ref, f32[128,3,128]{2,1,0:T(4,128)} %copy.27.nrm_ref, f32[128,128]{1,0:T(8,128)} %curv_ref.1, s32[128,1]{1,0:T(8,128)} %copy.28.cnt_ref), custom_call_target="tpu_custom_call" | custom-call | tf_op jit(solution)/shard_map/gather_blocks/pallas_call | solution.py:242
  51.2 17.0 %pairs.1.v_ref = f32[4,3,128,128]{3,2,1,0:T(8,128)} custom-call(s32[1,512]{1,0:T(1,128)} %tgt_ref.1, s32[1,512]{1,0:T(1,128)} %src_ref.1, s32[1]{0:T(128)S(6)} %copy.30.count_ref, f32[4,3,128,128]{3,2,1,0:T(8,128)} %get-tuple-element.7.t_ref, f32[4,6,128,128]{3,2,1,0:T(8,128)} %get-tuple-element.8.s_ref), custom_call_target="tpu_custom_call" | custom-call | tf_op jit(solution)/shard_map/pairs/pallas_call | solution.py:250
  68.1 70.2 %to_owners.1 = f32[128,3,128]{2,1,0:T(4,128)} custom-call(s32[256]{0:T(256)} %select_reduce_fusion.2.pack_ref, s32[128]{0:T(128)} %multiply_add_fusion.unpack_ref, s32[128]{0:T(128)} %reshape.113.cnt_ref, f32[4,3,128,128]{3,2,1,0:T(8,128)} %pairs.1.v_ref), custom_call_target="tpu_custom_call" | custom-call | tf_op jit(solution)/shard_map/to_owners/pallas_call | solution.py:258
  138.3 1.6 %copy.29 = f32[128,3,128]{2,0,1:T(8,128)} copy(f32[128,3,128]{2,1,0:T(4,128)} %to_owners.1) | data formatting | bytes 393216 | tf_op jit(solution)/shard_map/to_owners/pallas_call | solution.py:258
  (4 shorter events, 0.0 us)
Async XLA Ops:
  0.0 10.9 %copy-start = (f32[128,3,128]{2,0,1:T(8,128)S(1)}, f32[128,3,128]{2,0,1:T(8,128)}, u32[]{:S(2)}) copy-start(f32[128,3,128]{2,0,1:T(8,128)} %param.10) | copy-start | bytes 589828

commit v3 on v2

--- a/solution.py
+++ b/solution.py
@@ -15,7 +15,7 @@
 SMEM = pl.BlockSpec(memory_space=pltpu.SMEM)
 
 
-unroll = 4
+unroll = 16
 
 
 def gather_kernel(nrow, ncol, pos_ref, nrm_ref, curv_ref, cnt_ref, t_ref, s_ref, tsend, trecv, ssend, srecv):
@@ -34,18 +34,48 @@
         s_ref[row, 3 + k] = scale * nrm_ref[:, k, :]
     pl.semaphore_wait(barrier, nrow + ncol - 2)
     copies = []
-    for d in range(1, nrow):
-        copies.append(pltpu.make_async_remote_copy(
-            src_ref=s_ref.at[row], dst_ref=s_ref.at[row],
-            send_sem=ssend.at[d - 1], recv_sem=srecv.at[d - 1],
-            device_id={"row": lax.rem(row + d, nrow)}, device_id_type=MESH))
     for d in range(1, ncol):
         copies.append(pltpu.make_async_remote_copy(
             src_ref=t_ref.at[col], dst_ref=t_ref.at[col],
             send_sem=tsend.at[d - 1], recv_sem=trecv.at[d - 1],
             device_id={"col": lax.rem(col + d, ncol)}, device_id_type=MESH))
-    for copy in copies:
-        copy.start()
+
+    def relay(way, step):
+        block = jnp.clip(row - way * step, 0, nrow - 1)
+        to = jnp.clip(row + way, 0, nrow - 1)
+        at = step if way > 0 else nrow - 1 + step
+        return pltpu.make_async_remote_copy(
+            src_ref=s_ref.at[block], dst_ref=s_ref.at[block],
+            send_sem=ssend.at[at], recv_sem=srecv.at[at],
+            device_id={"row": to}, device_id_type=MESH)
+
+    def sends(way, step):
+        return (row < nrow - 1) & (row >= step) if way > 0 else (row > 0) & (row + step < nrow)
+
+    def receives(way, step):
+        return row >= step + 1 if way > 0 else row + step + 1 < nrow
+
+    for step in range(nrow - 1):
+        for way in (1, -1):
+            if step > 0:
+                @pl.when(receives(way, step - 1))
+                def _():
+                    relay(way, step - 1).wait_recv()
+
+            @pl.when(sends(way, step))
+            def _():
+                relay(way, step).start()
+        if step == 0:
+            for copy in copies:
+                copy.start()
+    for way in (1, -1):
+        @pl.when(receives(way, nrow - 2))
+        def _():
+            relay(way, nrow - 2).wait_recv()
+        for step in range(nrow - 1):
+            @pl.when(sends(way, step))
+            def _():
+                relay(way, step).wait_send()
     for copy in copies:
         copy.wait()
 
@@ -243,7 +273,7 @@
         functools.partial(gather_kernel, nrow, ncol),
         out_shape=(jax.ShapeDtypeStruct((ncol, 3, local, nodes), f32), jax.ShapeDtypeStruct((nrow, 6, local, nodes), f32)),
         in_specs=[VMEM] * 4, out_specs=(VMEM, VMEM),
-        scratch_shapes=[dma((ncol - 1,)), dma((ncol - 1,)), dma((nrow - 1,)), dma((nrow - 1,))],
+        scratch_shapes=[dma((ncol - 1,)), dma((ncol - 1,)), dma((2 * nrow - 2,)), dma((2 * nrow - 2,))],
         compiler_params=pltpu.CompilerParams(collective_id=0, has_side_effects=True, vmem_limit_bytes=56 << 20),
         name="gather_blocks",
     )(positions, normals, curvature, home_counts[:, None])

time: 142 us -> 107 us (0.75); the launches traced: 140 us -> 108 us
  Pallas kernels: 127 us -> 94.2 us
    pallas_call x1, Pallas kernels: 70.2 us -> 51.5 us  [per_device(): pl.pallas_call(functools.partial(home_kernel, nrow, ncol, cap), out_shape...]
    pallas_call x1, Pallas kernels: 39.5 us -> 30.3 us  [per_device(): pl.pallas_call(functools.partial(gather_kernel, nrow, ncol), out_shape=(j...]
    pallas_call x1, Pallas kernels: 17 us -> 12.3 us  [per_device(): pl.pallas_call(pair_kernel, out_shape=jax.ShapeDtypeStruct((ncol, 3, loca...]
where the time goes in v3:
time: 107 us; the launch traced here: 108 us
  Pallas kernels  94.2 us (88%)
  local copies, waits for them, and re-layouts  8.5 us (8%)
  other arithmetic  4.08 us (4%)
    pallas_call x1, Pallas kernels, per_device(): pl.pallas_call(functools.partial(home_kernel, nrow, ncol, cap), out_shape...  51.5 us
    pallas_call x1, Pallas kernels, per_device(): pl.pallas_call(functools.partial(gather_kernel, nrow, ncol), out_shape=(j...  30.3 us
    pallas_call x1, Pallas kernels, per_device(): pl.pallas_call(pair_kernel, out_shape=jax.ShapeDtypeStruct((ncol, 3, loca...  12.3 us
    unnamed x6, local copies, waits for them, and re-layouts  4.25 us

profile of v3, /device:TPU:15, one launch (start us, length us, event | category | flops | bytes accessed | tf_op | source)
XLA Modules:
  0.0 107.6 jit_solution(8581879192822139576)
XLA Ops:
  0.0 0.0 copy-start
  0.7 0.7 broadcast_compare_fusion
  1.4 0.1 convert_reduce_fusion
  1.5 1.3 %select_reduce_fusion = (s32[16,8]{1,0:T(8,128)S(1)}, s32[16,8]{1,0:T(8,128)S(1)}) fusion(s32[256,8]{0,1:T(8,128)} %param.15, pred[16,256]{1,0:T(8,128)(4,1)S(1)} %fusion.4, s32[256,8]{0,1:T(8,128)} %param.16), kind=kLoop, calls=%fused_computation.7 | loop fusion | flops 130816 | bytes 21504 | tf_op jit(solution)/shard_map/reduce_sum | solution.py:265
  2.9 0.7 reshape.113.cnt_ref
  3.5 0.1 reshape.112
  3.6 0.2 convert_reduce_fusion.1
  3.8 0.5 multiply_add_fusion.unpack_ref
  4.4 0.8 copy.25
  5.2 0.1 broadcast_in_dim.102
  5.3 0.8 copy.24
  6.1 0.1 eq.78
  6.2 0.8 broadcast_in_dim.92
  7.0 0.1 broadcast_in_dim.93
  7.1 0.3 fusion.1
  7.5 0.2 convert_reduce_fusion.2
  7.6 0.7 select_reduce_fusion.2.pack_ref
  8.3 0.7 copy.28.cnt_ref
  9.1 1.8 %copy.26.pos_ref = f32[128,3,128]{2,1,0:T(4,128)} copy(f32[128,3,128]{2,0,1:T(8,128)} %param.9) | data formatting | bytes 393216 | tf_op args[0]
  10.9 0.0 copy-done
  10.9 0.8 copy.27.nrm_ref
  11.7 30.3 %gather_blocks.1 = (f32[4,3,128,128]{3,2,1,0:T(8,128)}, f32[4,6,128,128]{3,2,1,0:T(8,128)}) custom-call(f32[128,3,128]{2,1,0:T(4,128)} %copy.26.pos_ref, f32[128,3,128]{2,1,0:T(4,128)} %copy.27.nrm_ref, f32[128,128]{1,0:T(8,128)} %curv_ref.1, s32[128,1]{1,0:T(8,128)} %copy.28.cnt_ref), custom_call_target="tpu_custom_call" | custom-call | tf_op jit(solution)/shard_map/gather_blocks/pallas_call | solution.py:272
  42.1 12.3 %pairs.1.v_ref = f32[4,3,128,128]{3,2,1,0:T(8,128)} custom-call(s32[1,512]{1,0:T(1,128)} %tgt_ref.1, s32[1,512]{1,0:T(1,128)} %src_ref.1, s32[1]{0:T(128)S(6)} %copy.30.count_ref, f32[4,3,128,128]{3,2,1,0:T(8,128)} %get-tuple-element.7.t_ref, f32[4,6,128,128]{3,2,1,0:T(8,128)} %get-tuple-element.8.s_ref), custom_call_target="tpu_custom_call" | custom-call | tf_op jit(solution)/shard_map/pairs/pallas_call | solution.py:280
  54.4 51.5 %to_owners.1 = f32[128,3,128]{2,1,0:T(4,128)} custom-call(s32[256]{0:T(256)} %select_reduce_fusion.2.pack_ref, s32[128]{0:T(128)} %multiply_add_fusion.unpack_ref, s32[128]{0:T(128)} %reshape.113.cnt_ref, f32[4,3,128,128]{3,2,1,0:T(8,128)} %pairs.1.v_ref), custom_call_target="tpu_custom_call" | custom-call | tf_op jit(solution)/shard_map/to_owners/pallas_call | solution.py:288
  105.9 1.6 %copy.29 = f32[128,3,128]{2,0,1:T(8,128)} copy(f32[128,3,128]{2,1,0:T(4,128)} %to_owners.1) | data formatting | bytes 393216 | tf_op jit(solution)/shard_map/to_owners/pallas_call | solution.py:288
  (4 shorter events, 0.0 us)
Async XLA Ops:
  0.0 10.9 %copy-start = (f32[128,3,128]{2,0,1:T(8,128)S(1)}, f32[128,3,128]{2,0,1:T(8,128)}, u32[]{:S(2)}) copy-start(f32[128,3,128]{2,0,1:T(8,128)} %param.10) | copy-start | bytes 589828

commit v4 on v3

--- a/solution.py
+++ b/solution.py
@@ -15,7 +15,7 @@
 SMEM = pl.BlockSpec(memory_space=pltpu.SMEM)
 
 
-unroll = 16
+unroll = 32
 
 
 def gather_kernel(nrow, ncol, pos_ref, nrm_ref, curv_ref, cnt_ref, t_ref, s_ref, tsend, trecv, ssend, srecv):
@@ -171,7 +171,7 @@
     lax.fori_loop(0, (count + unroll - 1) // unroll, many, 0)
 
 
-def home_kernel(nrow, ncol, cap, pack_ref, unpack_ref, cnt_ref, v_ref, out_ref, got, home, outg, arr, vsend, vrecv, asend, arecv):
+def home_kernel(nrow, ncol, cap, pack_ref, from_ref, rank_ref, cnt_ref, v_ref, out_ref, got, part, home, outg, arr, vsend, vrecv, asend, arecv):
     row, col = lax.axis_index("row"), lax.axis_index("col")
     local = out_ref.shape[0]
     devs = nrow * ncol
@@ -185,21 +185,37 @@
     for d in range(1, devs):
         pl.semaphore_signal(barrier, inc=1, device_id=peer(d), device_id_type=MESH)
     pl.semaphore_wait(barrier, devs - 1)
-    copies = []
-    for d in range(1, ncol):
-        to = lax.rem(col + d, ncol)
-        copies.append(pltpu.make_async_remote_copy(
-            src_ref=v_ref.at[to], dst_ref=got.at[d - 1], send_sem=vsend.at[d - 1], recv_sem=vrecv.at[d - 1],
-            device_id={"col": to}, device_id_type=MESH))
-    for copy in copies:
+    half = ncol // 2
+    core = lax.rem(col, 2)
+    mine_x = col // 2
+    within, across = [], []
+    for d in [*range(1, half), 0]:
+        x = lax.rem(mine_x + d, half)
+        within.append(pltpu.make_async_remote_copy(
+            src_ref=v_ref.at[2 * x + 1 - core], dst_ref=got.at[d], send_sem=vsend.at[d], recv_sem=vrecv.at[d],
+            device_id={"col": col + 1 - 2 * core}, device_id_type=MESH))
+    for copy in within:
         copy.start()
-    for copy in copies:
-        copy.wait()
+    for d in range(1, half):
+        to = 2 * lax.rem(mine_x + d, half) + core
+        within[d - 1].wait_recv()
+        part[d - 1] = v_ref[to] + got[d]
+        copy = pltpu.make_async_remote_copy(
+            src_ref=part.at[d - 1], dst_ref=got.at[half + d - 1],
+            send_sem=vsend.at[half + d - 1], recv_sem=vrecv.at[half + d - 1],
+            device_id={"col": to}, device_id_type=MESH)
+        copy.start()
+        across.append(copy)
+    within[half - 1].wait_recv()
+    for copy in across:
+        copy.wait_recv()
     for k in range(3):
-        mine = v_ref[col, k]
-        for d in range(1, ncol):
-            mine = mine + got[d - 1, k]
+        mine = v_ref[col, k] + got[0, k]
+        for d in range(1, half):
+            mine = mine + got[half + d - 1, k]
         home[:, k, :] = mine
+    for copy in within + across:
+        copy.wait_send()
 
     def pack(p, carry):
         for j in range(cap):
@@ -225,10 +241,10 @@
     def unpack(i, carry):
         for u in range(8):
             n = i * 8 + u
-            at = unpack_ref[n]
+            at, place = from_ref[n], rank_ref[n]
             live = slots < cnt_ref[n]
             for k in range(3):
-                out_ref[n, k:k + 1, :] = jnp.where(live, arr[at // cap, k, pl.ds(lax.rem(at, cap), 1), :], 0.0)
+                out_ref[n, k:k + 1, :] = jnp.where(live, arr[at, k, pl.ds(place, 1), :], 0.0)
         return carry
 
     lax.fori_loop(0, local // 8, unpack, 0)
@@ -265,7 +281,7 @@
     owned_counts = jnp.sum(jnp.where(chosen[:, :, None], node_counts[None], 0), axis=1, dtype=ints).reshape(-1)
     anchor = owned_clusters // local
     before = (anchor[None, :] == anchor[:, None]) & (owned_clusters[None, :] < owned_clusters[:, None])
-    unpack = anchor * cap + jnp.sum(before, axis=1, dtype=ints)
+    place_in = jnp.sum(before, axis=1, dtype=ints)
 
     dma = pltpu.SemaphoreType.DMA
     f32 = jnp.float32
@@ -288,15 +304,16 @@
     return pl.pallas_call(
         functools.partial(home_kernel, nrow, ncol, cap),
         out_shape=jax.ShapeDtypeStruct((local, 3, nodes), f32),
-        in_specs=[SMEM] * 3 + [VMEM], out_specs=VMEM,
+        in_specs=[SMEM] * 4 + [VMEM], out_specs=VMEM,
         scratch_shapes=[
-            pltpu.VMEM((ncol - 1, 3, local, nodes), f32), pltpu.VMEM((local, 8, nodes), f32),
+            pltpu.VMEM((ncol - 1, 3, local, nodes), f32), pltpu.VMEM((max(ncol // 2 - 1, 1), 3, local, nodes), f32),
+            pltpu.VMEM((local, 8, nodes), f32),
             pltpu.VMEM((devs, 3, cap, nodes), f32), pltpu.VMEM((devs, 3, cap, nodes), f32),
             dma((ncol - 1,)), dma((ncol - 1,)), dma((devs - 1,)), dma((devs - 1,)),
         ],
         compiler_params=pltpu.CompilerParams(collective_id=1, has_side_effects=True, vmem_limit_bytes=56 << 20),
         name="to_owners",
-    )(pack, unpack, owned_counts, speeds)
+    )(pack, anchor, place_in, owned_counts, speeds)
 
 
 def solution(mesh):

time: 107 us -> 99.1 us (0.926); the launches traced: 108 us -> 97.4 us
  Pallas kernels: 94.2 us -> 84 us
    pallas_call x1, Pallas kernels: 51.5 us -> 21.7 us  [per_device(): pl.pallas_call(functools.partial(home_kernel, nrow, ncol, cap), out_shape...]
    pallas_call x1, Pallas kernels: 12.3 us -> 32 us  [per_device(): pl.pallas_call(pair_kernel, out_shape=jax.ShapeDtypeStruct((ncol, 3, loca...]
    unnamed x6 -> x8, local copies, waits for them, and re-layouts: 4.25 us -> 4.26 us
where the time goes in v4:
time: 99.1 us; the launch traced here: 97.4 us
  Pallas kernels  84 us (85%)
  local copies, waits for them, and re-layouts  8.42 us (8%)
  other arithmetic  4.14 us (4%)
    pallas_call x1, Pallas kernels, per_device(): pl.pallas_call(pair_kernel, out_shape=jax.ShapeDtypeStruct((ncol, 3, loca...  32 us
    pallas_call x1, Pallas kernels, per_device(): pl.pallas_call(functools.partial(gather_kernel, nrow, ncol), out_shape=(j...  30.3 us
    pallas_call x1, Pallas kernels, per_device(): pl.pallas_call(functools.partial(home_kernel, nrow, ncol, cap), out_shape...  21.7 us
    unnamed x8, local copies, waits for them, and re-layouts  4.26 us

profile of v4, /device:TPU:15, one launch (start us, length us, event | category | flops | bytes accessed | tf_op | source)
XLA Modules:
  0.0 97.4 jit_solution(10821803387253262524)
XLA Ops:
  0.0 0.0 copy-start
  0.7 0.7 broadcast_compare_fusion
  1.4 0.1 convert_reduce_fusion
  1.5 1.3 %select_reduce_fusion = (s32[16,8]{1,0:T(8,128)S(1)}, s32[16,8]{1,0:T(8,128)S(1)}) fusion(s32[256,8]{0,1:T(8,128)} %param.15, pred[16,256]{1,0:T(8,128)(4,1)S(1)} %fusion.4, s32[256,8]{0,1:T(8,128)} %param.16), kind=kLoop, calls=%fused_computation.7 | loop fusion | flops 130816 | bytes 21504 | tf_op jit(solution)/shard_map/reduce_sum | solution.py:281
  2.9 0.6 reshape.113.cnt_ref
  3.5 0.1 reshape.112
  3.6 0.0 copy-start.1
  3.6 0.8 convert_reduce_fusion.1.rank_ref
  4.3 0.8 copy.25
  5.2 0.1 broadcast_in_dim.102
  5.3 0.8 copy.24
  6.1 0.1 eq.78
  6.2 0.8 broadcast_in_dim.92
  7.0 0.1 broadcast_in_dim.93
  7.1 0.3 fusion.1
  7.4 0.2 convert_reduce_fusion.2
  7.6 0.7 select_reduce_fusion.2.pack_ref
  8.3 0.7 copy.28.cnt_ref
  9.1 1.8 %copy.26.pos_ref = f32[128,3,128]{2,1,0:T(4,128)} copy(f32[128,3,128]{2,0,1:T(8,128)} %param.9) | data formatting | bytes 393216 | tf_op args[0]
  10.8 0.0 copy-done
  10.8 0.8 copy.27.nrm_ref
  11.7 30.3 %gather_blocks.1 = (f32[4,3,128,128]{3,2,1,0:T(8,128)}, f32[4,6,128,128]{3,2,1,0:T(8,128)}) custom-call(f32[128,3,128]{2,1,0:T(4,128)} %copy.26.pos_ref, f32[128,3,128]{2,1,0:T(4,128)} %copy.27.nrm_ref, f32[128,128]{1,0:T(8,128)} %curv_ref.1, s32[128,1]{1,0:T(8,128)} %copy.28.cnt_ref), custom_call_target="tpu_custom_call" | custom-call | tf_op jit(solution)/shard_map/gather_blocks/pallas_call | solution.py:288
  42.0 32.0 %pairs.1.v_ref = f32[4,3,128,128]{3,2,1,0:T(8,128)} custom-call(s32[1,512]{1,0:T(1,128)} %tgt_ref.1, s32[1,512]{1,0:T(1,128)} %src_ref.1, s32[1]{0:T(128)S(6)} %copy.30.count_ref, f32[4,3,128,128]{3,2,1,0:T(8,128)} %get-tuple-element.7.t_ref, f32[4,6,128,128]{3,2,1,0:T(8,128)} %get-tuple-element.8.s_ref), custom_call_target="tpu_custom_call" | custom-call | tf_op jit(solution)/shard_map/pairs/pallas_call | solution.py:296
  74.0 0.0 copy-done.1
  74.0 21.7 %to_owners.1 = f32[128,3,128]{2,1,0:T(4,128)} custom-call(s32[256]{0:T(256)} %select_reduce_fusion.2.pack_ref, s32[128]{0:T(128)} %copy-done.1, s32[128]{0:T(128)} %convert_reduce_fusion.1.rank_ref, s32[128]{0:T(128)} %reshape.113.cnt_ref, f32[4,3,128,128]{3,2,1,0:T(8,128)} %pairs.1.v_ref), custom_call_target="tpu_custom_call" | custom-call | tf_op jit(solution)/shard_map/to_owners/pallas_call | solution.py:304
  95.7 1.6 %copy.29 = f32[128,3,128]{2,0,1:T(8,128)} copy(f32[128,3,128]{2,1,0:T(4,128)} %to_owners.1) | data formatting | bytes 393216 | tf_op jit(solution)/shard_map/to_owners/pallas_call | solution.py:304
  (4 shorter events, 0.0 us)
Async XLA Ops:
  0.0 10.8 %copy-start = (f32[128,3,128]{2,0,1:T(8,128)S(1)}, f32[128,3,128]{2,0,1:T(8,128)}, u32[]{:S(2)}) copy-start(f32[128,3,128]{2,0,1:T(8,128)} %param.10) | copy-start | bytes 589828
  3.6 70.4 %copy-start.1 = (s32[128]{0:T(128)}, s32[128]{0:T(128)S(1)}, u32[]{:S(2)}) copy-start(s32[128]{0:T(128)S(1)} %and_select_fusion.from_ref) | copy-start | bytes 1540

commit v5 on v4

--- a/solution.py
+++ b/solution.py
@@ -28,10 +28,10 @@
     live = lax.broadcasted_iota(jnp.int32, curv_ref.shape, 1) < cnt_ref[...]
     scale = jnp.where(live, curv_ref[...], 0.0)
     for k in range(3):
-        coord = pos_ref[:, k, :]
+        coord = pos_ref[k]
         t_ref[col, k] = coord
         s_ref[row, k] = coord
-        s_ref[row, 3 + k] = scale * nrm_ref[:, k, :]
+        s_ref[row, 3 + k] = scale * nrm_ref[k]
     pl.semaphore_wait(barrier, nrow + ncol - 2)
     copies = []
     for d in range(1, ncol):
@@ -173,7 +173,7 @@
 
 def home_kernel(nrow, ncol, cap, pack_ref, from_ref, rank_ref, cnt_ref, v_ref, out_ref, got, part, home, outg, arr, vsend, vrecv, asend, arecv):
     row, col = lax.axis_index("row"), lax.axis_index("col")
-    local = out_ref.shape[0]
+    local = out_ref.shape[1]
     devs = nrow * ncol
     me = row * ncol + col
     barrier = pltpu.get_barrier_semaphore()
@@ -244,7 +244,7 @@
             at, place = from_ref[n], rank_ref[n]
             live = slots < cnt_ref[n]
             for k in range(3):
-                out_ref[n, k:k + 1, :] = jnp.where(live, arr[at, k, pl.ds(place, 1), :], 0.0)
+                out_ref[k, pl.ds(n, 1), :] = jnp.where(live, arr[at, k, pl.ds(place, 1), :], 0.0)
         return carry
 
     lax.fori_loop(0, local // 8, unpack, 0)
@@ -261,9 +261,9 @@
     here = local // per_drop
     ints = jnp.int32
 
-    flat_clusters = drop_clusters.reshape(-1)
-    flat_counts = node_counts.reshape(-1)
-    flat_owner = jnp.broadcast_to(drop_owner[:, None], (drops, per_drop)).reshape(-1)
+    flat_clusters = drop_clusters.T.reshape(-1)
+    flat_counts = node_counts.T.reshape(-1)
+    flat_owner = jnp.broadcast_to(drop_owner[None, :], (per_drop, drops)).reshape(-1)
     order = jnp.arange(local, dtype=ints)
     hit = (me * local + order)[:, None] == flat_clusters[None, :]
     home_counts = jnp.sum(jnp.where(hit, flat_counts[None, :], 0), axis=1, dtype=ints)
@@ -292,7 +292,7 @@
         scratch_shapes=[dma((ncol - 1,)), dma((ncol - 1,)), dma((2 * nrow - 2,)), dma((2 * nrow - 2,))],
         compiler_params=pltpu.CompilerParams(collective_id=0, has_side_effects=True, vmem_limit_bytes=56 << 20),
         name="gather_blocks",
-    )(positions, normals, curvature, home_counts[:, None])
+    )(jnp.transpose(positions, (1, 0, 2)), jnp.transpose(normals, (1, 0, 2)), curvature, home_counts[:, None])
     speeds = pl.pallas_call(
         pair_kernel,
         out_shape=jax.ShapeDtypeStruct((ncol, 3, local, nodes), f32),
@@ -301,9 +301,9 @@
         compiler_params=pltpu.CompilerParams(vmem_limit_bytes=56 << 20),
         name="pairs",
     )(pair_targets, pair_sources, pair_count, targets, sources)
-    return pl.pallas_call(
+    owned = pl.pallas_call(
         functools.partial(home_kernel, nrow, ncol, cap),
-        out_shape=jax.ShapeDtypeStruct((local, 3, nodes), f32),
+        out_shape=jax.ShapeDtypeStruct((3, local, nodes), f32),
         in_specs=[SMEM] * 4 + [VMEM], out_specs=VMEM,
         scratch_shapes=[
             pltpu.VMEM((ncol - 1, 3, local, nodes), f32), pltpu.VMEM((max(ncol // 2 - 1, 1), 3, local, nodes), f32),
@@ -314,6 +314,7 @@
         compiler_params=pltpu.CompilerParams(collective_id=1, has_side_effects=True, vmem_limit_bytes=56 << 20),
         name="to_owners",
     )(pack, anchor, place_in, owned_counts, speeds)
+    return jnp.transpose(owned, (1, 0, 2))
 
 
 def solution(mesh):

time: 99.1 us -> 97 us (0.979)
  the two profiles are of different devices: /device:TPU:15 before, /device:TPU:1 now
where the time goes in v5:
time: 97 us; the launch traced here: 96.8 us
  Pallas kernels  86.8 us (89%)
  local copies, waits for them, and re-layouts  5.14 us (5%)
  other arithmetic  4.13 us (4%)
    pallas_call x1, Pallas kernels, per_device(): pl.pallas_call(functools.partial(home_kernel, nrow, ncol, cap), out_shape...  36.7 us
    pallas_call x1, Pallas kernels, per_device(): pl.pallas_call(functools.partial(gather_kernel, nrow, ncol), out_shape=(j...  34.9 us
    pallas_call x1, Pallas kernels, per_device(): pl.pallas_call(pair_kernel, out_shape=jax.ShapeDtypeStruct((ncol, 3, loca...  15.2 us
    unnamed x7, local copies, waits for them, and re-layouts  3.71 us

profile of v5, /device:TPU:1, one launch (start us, length us, event | category | flops | bytes accessed | tf_op | source)
XLA Modules:
  0.0 96.8 jit_solution(6246586480567449983)
XLA Ops:
  0.7 0.7 broadcast_compare_fusion
  1.3 0.1 convert_reduce_fusion
  1.5 0.7 copy.17
  2.2 0.7 copy.19
  2.9 0.7 broadcast_bitcast_fusion
  3.6 0.3 fusion.1
  3.9 0.2 convert_reduce_fusion.2
  4.1 0.7 select_reduce_fusion.2.pack_ref
  4.8 1.3 %select_reduce_fusion = (s32[16,8]{1,0:T(8,128)S(1)}, s32[16,8]{1,0:T(8,128)S(1)}) fusion(s32[256,8]{0,1:T(8,128)} %param.15, pred[16,256]{1,0:T(8,128)(4,1)S(1)} %fusion.4, s32[256,8]{0,1:T(8,128)} %param.16), kind=kLoop, calls=%fused_computation.7 | loop fusion | flops 130816 | bytes 21504 | tf_op jit(solution)/shard_map/reduce_sum | solution.py:281
  6.1 0.6 reshape.113.cnt_ref
  6.7 0.1 reshape.112
  6.8 0.0 copy-start
  6.8 0.8 convert_reduce_fusion.1.rank_ref
  7.6 0.7 copy.16.cnt_ref
  8.4 34.9 %gather_blocks.1 = (f32[4,3,128,128]{3,2,1,0:T(8,128)}, f32[4,6,128,128]{3,2,1,0:T(8,128)}) custom-call(f32[3,128,128]{2,1,0:T(8,128)} %bitcast.14, f32[3,128,128]{2,1,0:T(8,128)} %bitcast.15, f32[128,128]{1,0:T(8,128)} %curv_ref.1, s32[128,1]{1,0:T(8,128)} %copy.16.cnt_ref), custom_call_target="tpu_custom_call" | custom-call | tf_op jit(solution)/shard_map/gather_blocks/pallas_call | solution.py:288
  43.3 15.2 %pairs.1.v_ref = f32[4,3,128,128]{3,2,1,0:T(8,128)} custom-call(s32[1,512]{1,0:T(1,128)} %tgt_ref.1, s32[1,512]{1,0:T(1,128)} %src_ref.1, s32[1]{0:T(128)S(6)} %copy.21.count_ref, f32[4,3,128,128]{3,2,1,0:T(8,128)} %get-tuple-element.7.t_ref, f32[4,6,128,128]{3,2,1,0:T(8,128)} %get-tuple-element.8.s_ref), custom_call_target="tpu_custom_call" | custom-call | tf_op jit(solution)/shard_map/pairs/pallas_call | solution.py:296
  58.5 0.0 copy-done
  58.5 36.7 %to_owners.1 = f32[3,128,128]{2,1,0:T(8,128)} custom-call(s32[256]{0:T(256)} %select_reduce_fusion.2.pack_ref, s32[128]{0:T(128)} %copy-done, s32[128]{0:T(128)} %convert_reduce_fusion.1.rank_ref, s32[128]{0:T(128)} %reshape.113.cnt_ref, f32[4,3,128,128]{3,2,1,0:T(8,128)} %pairs.1.v_ref), custom_call_target="tpu_custom_call" | custom-call | tf_op jit(solution)/shard_map/to_owners/pallas_call | solution.py:304
  95.2 1.6 %copy.22 = f32[128,3,128]{2,0,1:T(8,128)} copy(f32[128,3,128]{2,0,1:T(8,128)} %bitcast.13) | data formatting | bytes 393216
  (5 shorter events, 0.0 us)
Async XLA Ops:
  6.8 51.6 %copy-start = (s32[128]{0:T(128)}, s32[128]{0:T(128)S(1)}, u32[]{:S(2)}) copy-start(s32[128]{0:T(128)S(1)} %and_select_fusion.from_ref) | copy-start | bytes 1540
